TPU v7x, 32 devices: a whole 2x2x4 slice. The times are simulated.
32 devices in a mesh: dp: 4 (over x, core), seq: 8 (over z, y).
Axes of the slice: x: 2, y: 2, z: 4, core: 2. Of those that a mesh axis runs over, the one named last changes fastest.
Arguments:
- glu_out: bfloat16 [4, 1024, 1536], P('dp', 'seq'), may hold values from -6 to 6
- lengths: int32 [4], replicated, may hold values from 128 to 1024, as said below
- kernel: float32 [31, 1536], replicated, may hold values from -1 to 1
- gain: float32 [1536], replicated, may hold values from 0.25 to 1.75
- bias: float32 [1536], replicated, may hold values from -3 to 3
- weight: bfloat16 [1536, 1536], P(('dp', 'seq')), may hold values from -0.15625 to 0.15625
- master: float32 [1536, 1536], P(('dp', 'seq')), may hold values from -0.15625 to 0.15625
- moment_one: float32 [1536, 1536], P(('dp', 'seq')), may hold values from -120 to 120
- moment_two: float32 [1536, 1536], P(('dp', 'seq')), may hold values from 100 to 100000
- cotangent: bfloat16 [4, 1024, 1536], P('dp', 'seq'), may hold values from -6 to 6
Outputs:
- module_out: bfloat16 [4, 1024, 1536], P('dp', 'seq')
- input_grad: bfloat16 [4, 1024, 1536], P('dp', 'seq')
- kernel_grad: float32 [31, 1536], replicated
- gain_grad: float32 [1536], replicated
- bias_grad: float32 [1536], replicated
- new_master: float32 [1536, 1536], P(('dp', 'seq'))
- new_one: float32 [1536, 1536], P(('dp', 'seq'))
- new_two: float32 [1536, 1536], P(('dp', 'seq'))
Inputs may be any that keep to these rules, and one draw needn't show every extreme that they name: `lengths`: in every draw one stream has all 1024 frames valid; each other stream has between 128 and 341 valid frames.
All inputs are finite; a program needn't handle non-finite values.
Results may differ from a plain program's by a relative error of at most 0.0049.
Values may be sent and summed in bfloat16 or wider, within the bound.
A program may use at most 64 MiB of HBM per device.

v0:
```python
import jax
import jax.numpy as jnp
from jax import lax
from jax.sharding import PartitionSpec as P

KERNEL = 31
HALF = 15


beta_one = 0.9
beta_two = 0.999
adam_rate = 0.001
adam_eps = 1e-08
norm_eps = 1e-05
first_fix = 0.9999734386011124
second_fix = 0.09520785288629043


def with_halo(block, sides, width):
    for axis, dim in sides:
        count = lax.axis_size(axis)
        forward = [(i, i + 1) for i in range(count - 1)]
        backward = [(target, source) for source, target in forward]
        low = lax.ppermute(
            lax.slice_in_dim(block, block.shape[dim] - width, None, axis=dim), axis, forward
        )
        high = lax.ppermute(lax.slice_in_dim(block, 0, width, axis=dim), axis, backward)
        block = jnp.concatenate([low, block, high], axis=dim)
    return block


def on_device(
    glu_out, lengths, kernel, gain, bias, weight, master, moment_one, moment_two, cotangent
):
    frames = glu_out.shape[1]
    stream = lax.axis_index("dp")
    shard = lax.axis_index("seq")
    positions = shard * frames + jnp.arange(frames, dtype=jnp.int32)
    valid = (positions < lengths[stream])[:, None]
    count = jnp.sum(lengths).astype(jnp.float32)
    masked = jnp.where(valid, glu_out[0], jnp.zeros((), glu_out.dtype))
    padded = with_halo(masked, (("seq", 0),), HALF).astype(jnp.float32)
    conv_out = jnp.zeros((frames, masked.shape[1]), jnp.float32)
    for tap in range(KERNEL):
        conv_out = conv_out + kernel[tap] * padded[tap : tap + frames]
    total = lax.psum(jnp.sum(jnp.where(valid, conv_out, 0.0), axis=0), ("dp", "seq"))
    channel_mean = total / count
    deviation = jnp.where(valid, conv_out - channel_mean, 0.0)
    spread = lax.psum(jnp.sum(deviation * deviation, axis=0), ("dp", "seq"))
    channel_var = spread / count
    inv_std = lax.rsqrt(channel_var + norm_eps)
    standard = (conv_out - channel_mean) * inv_std
    scaled = gain * standard + bias
    logistic = jax.nn.sigmoid(scaled)
    hidden = (scaled * logistic).astype(jnp.bfloat16)
    grad_out = jnp.where(valid, cotangent[0], jnp.zeros((), cotangent.dtype))
    columns = hidden
    product = jnp.dot(
        columns,
        lax.all_gather(weight, ("dp", "seq"), axis=0, tiled=True),
        preferred_element_type=jnp.float32,
    )
    hidden_grad = lax.dot_general(
        grad_out,
        lax.all_gather(weight, ("dp", "seq"), axis=0, tiled=True),
        (((1,), (1,)), ((), ())),
        preferred_element_type=jnp.float32,
    )
    module_out = jnp.where(valid, product, 0.0).astype(jnp.bfloat16)
    scaled_grad = hidden_grad * logistic * (1.0 + scaled * (1.0 - logistic))
    gain_grad, bias_grad = lax.psum(
        (jnp.sum(scaled_grad * standard, axis=0), jnp.sum(scaled_grad, axis=0)), ("dp", "seq")
    )
    conv_grad = jnp.where(
        valid,
        inv_std
        * (gain * scaled_grad - gain * bias_grad / count - standard * gain * gain_grad / count),
        0.0,
    )
    grad_pad = with_halo(conv_grad, (("seq", 0),), HALF)
    flipped = jnp.zeros((frames, conv_grad.shape[1]), jnp.float32)
    for tap in range(KERNEL):
        flipped = flipped + kernel[tap] * grad_pad[2 * HALF - tap : 2 * HALF - tap + frames]
    input_grad = jnp.where(valid, flipped, 0.0).astype(jnp.bfloat16)
    tap_rows = []
    for tap in range(KERNEL):
        tap_rows.append(jnp.sum(conv_grad * padded[tap : tap + frames], axis=0))
    kernel_grad = lax.psum(jnp.stack(tap_rows), ("dp", "seq"))
    columns = hidden
    weight_grad = lax.psum_scatter(
        lax.dot_general(
            columns, grad_out, (((0,), (0,)), ((), ())), preferred_element_type=jnp.float32
        ),
        ("dp", "seq"),
        scatter_dimension=0,
        tiled=True,
    )
    new_one = beta_one * moment_one + (1.0 - beta_one) * weight_grad
    new_two = beta_two * moment_two + (1.0 - beta_two) * weight_grad * weight_grad
    new_master = master - adam_rate * (new_one / first_fix) / (
        jnp.sqrt(new_two / second_fix) + adam_eps
    )
    return (
        module_out[None],
        input_grad[None],
        kernel_grad,
        gain_grad,
        bias_grad,
        new_master,
        new_one,
        new_two,
    )


def solution(mesh):
    return jax.shard_map(
        on_device,
        mesh=mesh,
        in_specs=(
            P("dp", "seq", None),
            P(),
            P(),
            P(),
            P(),
            P(("dp", "seq"), None),
            P(("dp", "seq"), None),
            P(("dp", "seq"), None),
            P(("dp", "seq"), None),
            P("dp", "seq", None),
        ),
        out_specs=(
            P("dp", "seq", None),
            P("dp", "seq", None),
            P(),
            P(),
            P(),
            P(("dp", "seq"), None),
            P(("dp", "seq"), None),
            P(("dp", "seq"), None),
        ),
        check_vma=False,
    )
```

profile of v0, /device:TPU:10, one launch (start us, length us, event | category | flops | bytes accessed | tf_op | source)
XLA Modules:
  0.0 389.7 jit_solution(2780016820714955220)
XLA Ops:
  7.2 0.0 all-gather.2.cloned.1.call-start
  7.2 0.7 all-gather.2.cloned.1.call-update
  7.9 0.0 reduce-scatter.2.cloned.1.call-start
  8.0 1.2 dynamic_slice.3
  9.2 0.7 add_compare_fusion
  9.9 0.0 copy-start.23
  9.9 1.1 bitcast_select_fusion.1
  11.0 3.4 collective-permute-start
  14.4 3.3 collective-permute-start.1
  17.7 1.8 slice_reduce_fusion.30
  19.5 1.5 slice_reduce_fusion.29
  21.0 0.0 copy-start.5
  21.1 0.0 copy-start.7
  21.1 0.0 copy-start.17
  21.1 0.0 copy-start.19
  21.1 1.3 reduce_sum.325
  23.1 0.1 maximum_convert_fusion
  23.2 0.0 copy-start
  23.2 0.0 copy-start.4
  23.3 0.0 copy-start.21
  23.3 3.2 select_reduce_fusion
  26.5 41.0 %psum.35 = f32[1536]{0:T(1024)S(1)} all-reduce(f32[1536]{0:T(1024)S(1)} %get-tuple-element.78), channel_id=1, replica_groups=mesh['dp'=4,'seq'=8] {'dp','seq'}, use_global_device_ids=true, to_apply=%region_1.2 | all-reduce | flops 1536 | bytes 12288 | tf_op jit(solution)/shard_map/psum | solution.py:46
  67.5 0.2 multiply_reduce_fusion.32
  67.7 40.1 %psum.36 = f32[1536]{0:T(1024)S(1)} all-reduce(f32[1536]{0:T(1024)S(1)} %multiply_reduce_fusion.32), channel_id=1, replica_groups=mesh['dp'=4,'seq'=8] {'dp','seq'}, use_global_device_ids=true, to_apply=%region_4.5 | all-reduce | flops 1536 | bytes 12288 | tf_op jit(solution)/shard_map/psum | solution.py:49
  107.8 5.1 %fusion.95 = f32[1536,1536]{1,0:T(8,128)} fusion(bf16[1,128,1536]{2,1,0:T(8,128)(2,1)S(1)} %copy-done, pred[128]{0:T(512)(128)(4,1)S(1)} %add_compare_fusion, f32[128,1536]{1,0:T(8,128)S(1)} %get-tuple-element.79, f32[1536]{0:T(1024)S(1)} %copy-done.21, f32[1536]{0:T(1024)S(1)} %add_rsqrt_fusion, f32[1536]{0:T(1024)S(1)} %broadcast_divide_fusion, ...), kind=kOutput, calls=%fused_computation.200 | convolution fusion | flops 605945856 | bytes 10641536 | tf_op jit(solution)/shard_map/dot_general | solution.py:91
  112.9 0.0 reduce-scatter.2.cloned.1.call-update
  112.9 0.0 all-reduce.3.cloned.1.call-start
  113.0 0.0 all-gather.2.cloned.1.call-done
  113.0 4.1 %fusion.98 = (f32[1536]{0:T(1024)S(1)}, f32[1536]{0:T(1024)S(1)}, f32[128,1536]{1,0:T(8,128)S(1)}) fusion(f32[1536]{0:T(1024)S(1)} %add_rsqrt_fusion, f32[128,1536]{1,0:T(8,128)S(1)} %get-tuple-element.79, f32[1536]{0:T(1024)S(1)} %broadcast_divide_fusion, f32[1536]{0:T(1024)S(1)} %copy-done.21, f32[1536]{0:T(1024)S(1)} %copy-done.4, ...), kind=kOutput, calls=%fused_computation.238 | convolution fusion | flops 607122432 | bytes 6721664 | tf_op jit(solution)/shard_map/dot_general | solution.py:63
  117.1 40.2 %all-reduce = (f32[1536]{0:T(1024)}, f32[1536]{0:T(1024)S(1)}) all-reduce(f32[1536]{0:T(1024)S(1)} %get-tuple-element.40, f32[1536]{0:T(1024)S(1)} %get-tuple-element.39), channel_id=1, replica_groups=mesh['dp'=4,'seq'=8] {'dp','seq'}, use_global_device_ids=true, to_apply=%region_8.9 | all-reduce | flops 3072 | bytes 24576 | tf_op jit(solution)/shard_map/psum | solution.py:71
  157.4 0.6 copy-done.25
  158.0 3.0 multiply_reduce_fusion
  161.0 1.2 multiply_reduce_fusion.1
  162.7 3.6 collective-permute-start.2
  166.3 0.0 copy-start.6
  166.4 0.0 copy-start.20
  166.4 2.5 collective-permute-start.3
  168.9 2.8 stack.127
  171.7 0.0 all-reduce.3.cloned.1.call-update
  171.7 0.0 copy-start.1
  171.8 0.0 copy-start.2
  171.8 4.1 %fusion.2 = bf16[1,128,1536]{2,1,0:T(8,128)(2,1)} fusion(bf16[1536,1536]{1,0:T(8,128)(2,1)} %all-gather.2.cloned.1.call-done, pred[128]{0:T(512)(128)(4,1)S(1)} %copy-done.24, f32[128,1536]{1,0:T(8,128)S(1)} %get-tuple-element.79, f32[1536]{0:T(1024)S(1)} %copy-done.22, f32[1536]{0:T(1024)S(1)} %add_rsqrt_fusion, f32[1536]{0:T(1024)S(1)} %broadcast_divide_fusion, ...), kind=kOutput, calls=%fused_computation.32 | convolution fusion | flops 606142464 | bytes 5922944 | tf_op jit(solution)/shard_map/dot_general | solution.py:58
  175.9 0.3 collective-permute-done.3
  176.2 4.4 %fusion.93 = bf16[1,128,1536]{2,1,0:T(8,128)(2,1)} fusion(f32[128,1536]{1,0:T(8,128)S(1)} %get-tuple-element.77, f32[15,1536]{1,0:T(8,128)S(1)} %collective-permute-done.3, f32[1536]{0:T(1024)S(1)} %copy-done.18, f32[1536]{0:T(1024)S(1)} %copy-done.20, f32[1536]{0:T(1024)S(1)} %get-tuple-element.42, f32[1536]{0:T(1024)S(1)} %get-tuple-element.43, ...), kind=kLoop, calls=%fused_computation.196 | loop fusion | flops 18284544 | bytes 1554560 | tf_op jit(solution)/shard_map/broadcast_in_dim | solution.py:105
  180.6 69.7 %reduce-scatter.2.cloned.1.call-done = f32[48,1536]{1,0:T(8,128)} async-done(((f32[1536,1536]{1,0:T(8,128)}), f32[48,1536]{1,0:T(8,128)}) %reduce-scatter.2.cloned.1.call-update) | async-done | bytes 294928 | tf_op jit(solution)/shard_map/reduce_scatter | solution.py:90
  250.3 2.0 divide_subtract_fusion
  252.3 129.2 %all-reduce.3.cloned.1.call-done = f32[31,1536]{1,0:T(8,128)} async-done(((f32[31,1536]{1,0:T(8,128)}), f32[31,1536]{1,0:T(8,128)}) %all-reduce.3.cloned.1.call-update) | async-done | bytes 190480 | tf_op jit(solution)/shard_map/psum | solution.py:88
  381.5 1.6 copy.19
  (78 shorter events, 0.3 us)
Async XLA Ops:
  7.2 105.8 %all-gather.2.cloned.1.call-start = ((), (), s32[]{:S(2)}) async-start(), calls=%async_computation.1 | async-start | bytes 4866048 | tf_op jit(solution)/shard_map/all_gather | solution.py:60
  7.9 242.4 %reduce-scatter.2.cloned.1.call-start = ((), (), s32[]{:S(2)}) async-start(), calls=%async_computation.3 | async-start | bytes 9732096 | tf_op jit(solution)/shard_map/reduce_scatter | solution.py:90
  9.9 103.2 %copy-start.23 = (pred[128]{0:T(512)(128)(4,1)}, pred[128]{0:T(512)(128)(4,1)S(1)}, u32[]{:S(2)}) copy-start(pred[128]{0:T(512)(128)(4,1)S(1)} %add_compare_fusion) | copy-start | bytes 388
  11.0 12.1 %collective-permute-start = (bf16[15,1536]{1,0:T(8,128)(2,1)S(1)}, bf16[15,1536]{1,0:T(8,128)(2,1)S(1)}, u32[]{:S(2)}, u32[]{:S(2)}) collective-permute-start(bf16[15,1536]{1,0:T(8,128)(2,1)S(1)} %get-tuple-element.82), channel_id=1, source_target_pairs={{0,1},{1,2},{2,3},{3,4},{4,5},{5,6},{6,7},{8,9},{9,10},{10,11},{11... | collective-permute-start | bytes 138248 | tf_op jit(solution)/shard_map/ppermute | solution.py:24
  14.4 8.7 %collective-permute-start.1 = (bf16[15,1536]{1,0:T(8,128)(2,1)S(1)}, bf16[15,1536]{1,0:T(8,128)(2,1)S(1)}, u32[]{:S(2)}, u32[]{:S(2)}) collective-permute-start(bf16[15,1536]{1,0:T(8,128)(2,1)S(1)} %get-tuple-element.83), channel_id=1, source_target_pairs={{1,0},{2,1},{3,2},{4,3},{5,4},{6,5},{7,6},{9,8},{10,9},{11,10},{12... | collective-permute-start | bytes 138248 | tf_op jit(solution)/shard_map/ppermute | solution.py:27
  21.0 5.4 %copy-start.5 = (f32[1536]{0:T(1024)}, f32[1536]{0:T(1024)S(1)}, u32[]{:S(2)}) copy-start(f32[1536]{0:T(1024)S(1)} %get-tuple-element.64) | copy-start | bytes 18436
  21.1 5.4 %copy-start.7 = (f32[1536]{0:T(1024)}, f32[1536]{0:T(1024)S(1)}, u32[]{:S(2)}) copy-start(f32[1536]{0:T(1024)S(1)} %get-tuple-element.65) | copy-start | bytes 18436
  21.1 5.4 %copy-start.9 = (f32[1536]{0:T(1024)}, f32[1536]{0:T(1024)S(1)}, u32[]{:S(2)}) copy-start(f32[1536]{0:T(1024)S(1)} %get-tuple-element.66) | copy-start | bytes 18436
  21.1 5.4 %copy-start.11 = (f32[1536]{0:T(1024)}, f32[1536]{0:T(1024)S(1)}, u32[]{:S(2)}) copy-start(f32[1536]{0:T(1024)S(1)} %get-tuple-element.67) | copy-start | bytes 18436
  21.1 5.4 %copy-start.13 = (f32[1536]{0:T(1024)}, f32[1536]{0:T(1024)S(1)}, u32[]{:S(2)}) copy-start(f32[1536]{0:T(1024)S(1)} %get-tuple-element.68) | copy-start | bytes 18436
  21.1 5.4 %copy-start.15 = (f32[1536]{0:T(1024)}, f32[1536]{0:T(1024)S(1)}, u32[]{:S(2)}) copy-start(f32[1536]{0:T(1024)S(1)} %get-tuple-element.69) | copy-start | bytes 18436
  21.1 5.4 %copy-start.17 = (f32[1536]{0:T(1024)}, f32[1536]{0:T(1024)S(1)}, u32[]{:S(2)}) copy-start(f32[1536]{0:T(1024)S(1)} %get-tuple-element.70) | copy-start | bytes 18436
  21.1 5.4 %copy-start.19 = (f32[1536]{0:T(1024)}, f32[1536]{0:T(1024)S(1)}, u32[]{:S(2)}) copy-start(f32[1536]{0:T(1024)S(1)} %get-tuple-element.71) | copy-start | bytes 18436
  23.2 84.6 %copy-start = (bf16[1,128,1536]{2,1,0:T(8,128)(2,1)S(1)}, bf16[1,128,1536]{2,1,0:T(8,128)(2,1)}, u32[]{:S(2)}) copy-start(bf16[1,128,1536]{2,1,0:T(8,128)(2,1)} %param.19) | copy-start | bytes 1179652
  23.2 84.6 %copy-start.4 = (f32[1536]{0:T(1024)S(1)}, f32[1536]{0:T(1024)}, u32[]{:S(2)}) copy-start(f32[1536]{0:T(1024)} %param.13) | copy-start | bytes 18436
  23.3 84.5 %copy-start.21 = (f32[1536]{0:T(1024)S(1)}, f32[1536]{0:T(1024)}, u32[]{:S(2)}) copy-start(f32[1536]{0:T(1024)} %param.14) | copy-start | bytes 18436
  112.9 268.6 %all-reduce.3.cloned.1.call-start = ((), (), s32[]{:S(2)}) async-start(), calls=%async_computation.2 | async-start | bytes 393216 | tf_op jit(solution)/shard_map/psum | solution.py:88
  157.4 0.6 copy-start.25
  161.0 10.7 %copy-start.22 = (f32[1536]{0:T(1024)S(1)}, f32[1536]{0:T(1024)}, u32[]{:S(2)}) copy-start(f32[1536]{0:T(1024)} %param.14) | copy-start | bytes 18436
  161.0 10.7 %copy-start.24 = (pred[128]{0:T(512)(128)(4,1)S(1)}, pred[128]{0:T(512)(128)(4,1)}, u32[]{:S(2)}) copy-start(pred[128]{0:T(512)(128)(4,1)} %copy-done.23) | copy-start | bytes 388
  162.7 13.2 %collective-permute-start.2 = (f32[15,1536]{1,0:T(8,128)S(1)}, f32[15,1536]{1,0:T(8,128)S(1)}, u32[]{:S(2)}, u32[]{:S(2)}) collective-permute-start(f32[15,1536]{1,0:T(8,128)S(1)} %get-tuple-element.80), channel_id=1, source_target_pairs={{1,0},{2,1},{3,2},{4,3},{5,4},{6,5},{7,6},{9,8},{10,9},{11,10},{12... | collective-permute-start | bytes 276488 | tf_op jit(solution)/shard_map/ppermute | solution.py:27
  166.3 9.8 %copy-start.6 = (f32[1536]{0:T(1024)S(1)}, f32[1536]{0:T(1024)}, u32[]{:S(2)}) copy-start(f32[1536]{0:T(1024)} %copy-done.5) | copy-start | bytes 18436
  166.3 9.8 %copy-start.8 = (f32[1536]{0:T(1024)S(1)}, f32[1536]{0:T(1024)}, u32[]{:S(2)}) copy-start(f32[1536]{0:T(1024)} %copy-done.7) | copy-start | bytes 18436
  166.3 9.8 %copy-start.10 = (f32[1536]{0:T(1024)S(1)}, f32[1536]{0:T(1024)}, u32[]{:S(2)}) copy-start(f32[1536]{0:T(1024)} %copy-done.9) | copy-start | bytes 18436
  166.4 9.8 %copy-start.12 = (f32[1536]{0:T(1024)S(1)}, f32[1536]{0:T(1024)}, u32[]{:S(2)}) copy-start(f32[1536]{0:T(1024)} %copy-done.11) | copy-start | bytes 18436
  166.4 9.8 %copy-start.14 = (f32[1536]{0:T(1024)S(1)}, f32[1536]{0:T(1024)}, u32[]{:S(2)}) copy-start(f32[1536]{0:T(1024)} %copy-done.13) | copy-start | bytes 18436
  166.4 9.8 %copy-start.16 = (f32[1536]{0:T(1024)S(1)}, f32[1536]{0:T(1024)}, u32[]{:S(2)}) copy-start(f32[1536]{0:T(1024)} %copy-done.15) | copy-start | bytes 18436
  166.4 9.8 %copy-start.18 = (f32[1536]{0:T(1024)S(1)}, f32[1536]{0:T(1024)}, u32[]{:S(2)}) copy-start(f32[1536]{0:T(1024)} %copy-done.17) | copy-start | bytes 18436
  166.4 9.8 %copy-start.20 = (f32[1536]{0:T(1024)S(1)}, f32[1536]{0:T(1024)}, u32[]{:S(2)}) copy-start(f32[1536]{0:T(1024)} %copy-done.19) | copy-start | bytes 18436
  166.4 9.7 %collective-permute-start.3 = (f32[15,1536]{1,0:T(8,128)S(1)}, f32[15,1536]{1,0:T(8,128)S(1)}, u32[]{:S(2)}, u32[]{:S(2)}) collective-permute-start(f32[15,1536]{1,0:T(8,128)S(1)} %get-tuple-element.81), channel_id=1, source_target_pairs={{0,1},{1,2},{2,3},{3,4},{4,5},{5,6},{6,7},{8,9},{9,10},{10,11},{11... | collective-permute-start | bytes 276488 | tf_op jit(solution)/shard_map/ppermute | solution.py:24
  171.7 78.5 %copy-start.1 = (f32[48,1536]{1,0:T(8,128)S(1)}, f32[48,1536]{1,0:T(8,128)}, u32[]{:S(2)}) copy-start(f32[48,1536]{1,0:T(8,128)} %param.16) | copy-start | bytes 884740
  171.8 78.5 %copy-start.2 = (f32[48,1536]{1,0:T(8,128)S(1)}, f32[48,1536]{1,0:T(8,128)}, u32[]{:S(2)}) copy-start(f32[48,1536]{1,0:T(8,128)} %param.17) | copy-start | bytes 884740
  171.8 78.5 %copy-start.3 = (f32[48,1536]{1,0:T(8,128)S(1)}, f32[48,1536]{1,0:T(8,128)}, u32[]{:S(2)}) copy-start(f32[48,1536]{1,0:T(8,128)} %param.18) | copy-start | bytes 884740
Sparse Core Ops, SparseCore 0:
  10.9 65.8 all-gather.1
  113.0 137.2 reduce-scatter.1
  257.3 124.1 all-reduce.2
where the time goes:
time: 390 us
  waiting for transfers between devices  200 us (51%)
  blocking collectives  121 us (31%)
  other arithmetic  17.1 us (4%)
  between operations  15.1 us (4%)
  matrix products  13.3 us (3%)
  starting transfers between devices  13 us (3%)
  local copies, waits for them, and re-layouts  9.87 us (3%)
    psum x1, waiting for transfers between devices, on_device(): kernel_grad = lax.psum(jnp.stack(tap_rows), ('dp', 'seq'))  129 us
    reduce_scatter x1, waiting for transfers between devices, on_device(): lax.psum_scatter(lax.dot_general(columns, grad_out, (((0,), (0,)), ((), (...  69.7 us
    psum x1, blocking collectives, on_device(): lax.psum(jnp.sum(jnp.where(valid, conv_out, 0.0), axis=0), ('dp', 'seq'))  41 us
    psum x1, blocking collectives, on_device(): lax.psum((jnp.sum(scaled_grad * standard, axis=0), jnp.sum(scaled_grad, a...  40.2 us
    psum x1, blocking collectives, on_device(): spread = lax.psum(jnp.sum(deviation * deviation, axis=0), ('dp', 'seq'))  40.1 us
  transfers between devices with their start and end apart: 7, of which 3 were waited for; matrix products, arithmetic and copies ran while one was open for 10% of the time, Pallas kernels for 0%

commit v1 on v0

--- a/solution.py
+++ b/solution.py
@@ -1,6 +1,10 @@
+import functools
+
 import jax
 import jax.numpy as jnp
 from jax import lax
+from jax.experimental import pallas as pl
+from jax.experimental.pallas import tpu as pltpu
 from jax.sharding import PartitionSpec as P
 
 KERNEL = 31
@@ -27,6 +31,195 @@
         high = lax.ppermute(lax.slice_in_dim(block, 0, width, axis=dim), axis, backward)
         block = jnp.concatenate([low, block, high], axis=dim)
     return block
+
+
+MESH = pl.DeviceIdType.MESH
+LANES = 128
+AXES = ("dp", "seq")
+
+
+def greet(sizes):
+    barrier = pltpu.get_barrier_semaphore()
+    for axis in AXES:
+        me = lax.axis_index(axis)
+        for step in range(1, sizes[axis]):
+            pl.semaphore_signal(
+                barrier,
+                inc=1,
+                device_id={axis: lax.rem(me + step, sizes[axis])},
+                device_id_type=MESH,
+            )
+    pl.semaphore_wait(barrier, sizes["dp"] + sizes["seq"] - 2)
+
+
+def exchange(axis, size, source, target, send_sem, recv_sem):
+    me = lax.axis_index(axis)
+    copies = []
+    for step in range(1, size):
+        peer = lax.rem(me + step, size)
+        copy = pltpu.make_async_remote_copy(
+            src_ref=source(peer),
+            dst_ref=target(me),
+            send_sem=send_sem.at[step],
+            recv_sem=recv_sem.at[step],
+            device_id={axis: peer},
+            device_id_type=MESH,
+        )
+        copy.start()
+        copies.append(copy)
+    return copies
+
+
+def finish(copies):
+    for copy in copies:
+        copy.wait()
+
+
+def plain_sum(slots, count):
+    total = slots[0]
+    for i in range(1, count):
+        total = total + slots[i]
+    return total
+
+
+def moments(slots, frames, count):
+    half = slots.shape[1] // 2
+    sums = [slots[i][:half] for i in range(count)]
+    have = [frames[i] for i in range(count)]
+    total, spread, members = sums[0], slots[0][half:], have[0]
+    for i in range(1, count):
+        total, spread, members = total + sums[i], spread + slots[i][half:], members + have[i]
+    mean = total / jnp.maximum(members, 1.0)
+    for i in range(count):
+        off = sums[i] / jnp.maximum(have[i], 1.0) - mean
+        spread = spread + have[i] * off * off
+    return total, spread
+
+
+def small_kernel(sizes, joined, x_ref, *rest):
+    if joined:
+        dp_frames, seq_frames, *rest = rest
+    out_ref, first, second, send_a, recv_a, send_b, recv_b = rest
+    stream, shard = lax.axis_index("dp"), lax.axis_index("seq")
+    half = x_ref.shape[0] // 2
+    greet(sizes)
+    copies = exchange(
+        "dp", sizes["dp"], lambda p: x_ref, lambda m: first.at[m], send_a, recv_a
+    )
+    first[stream] = x_ref[...]
+    finish(copies)
+    if joined:
+        total, spread = moments(first, dp_frames, sizes["dp"])
+        second[shard, :half] = total
+        second[shard, half:] = spread
+    else:
+        second[shard] = plain_sum(first, sizes["dp"])
+    copies = exchange(
+        "seq",
+        sizes["seq"],
+        lambda p: second.at[shard],
+        lambda m: second.at[m],
+        send_b,
+        recv_b,
+    )
+    finish(copies)
+    if joined:
+        total, spread = moments(second, seq_frames, sizes["seq"])
+        out_ref[:half] = total
+        out_ref[half:] = spread
+    else:
+        out_ref[...] = plain_sum(second, sizes["seq"])
+
+
+def sems(sizes, axis):
+    return [pltpu.SemaphoreType.DMA((sizes[axis],))] * 2
+
+
+def small_reduce(rows, ident, frames=None):
+    sizes = {axis: lax.axis_size(axis) for axis in AXES}
+    flat = rows.reshape(-1, LANES)
+    args = [flat] if frames is None else [flat, *frames]
+    out = pl.pallas_call(
+        functools.partial(small_kernel, sizes, frames is not None),
+        out_shape=jax.ShapeDtypeStruct(flat.shape, jnp.float32),
+        in_specs=[pl.BlockSpec(memory_space=pltpu.VMEM)] * len(args),
+        out_specs=pl.BlockSpec(memory_space=pltpu.VMEM),
+        scratch_shapes=[
+            pltpu.VMEM((sizes["dp"], *flat.shape), jnp.float32),
+            pltpu.VMEM((sizes["seq"], *flat.shape), jnp.float32),
+            *sems(sizes, "dp"),
+            *sems(sizes, "seq"),
+        ],
+        compiler_params=pltpu.CompilerParams(collective_id=ident, has_side_effects=True),
+    )(*args)
+    return out.reshape(rows.shape)
+
+
+def wide_kernel(sizes, x_ref, out_ref, first, second, *sem):
+    stream, shard = lax.axis_index("dp"), lax.axis_index("seq")
+    greet(sizes)
+    copies = exchange(
+        "dp", sizes["dp"], lambda p: x_ref.at[p], lambda m: first.at[m], sem[0], sem[1]
+    )
+    first[stream] = x_ref[stream]
+    finish(copies)
+    first[stream] = plain_sum(first, sizes["dp"])
+    copies = exchange(
+        "seq",
+        sizes["seq"],
+        lambda p: first.at[stream, p],
+        lambda m: second.at[m],
+        sem[2],
+        sem[3],
+    )
+    second[shard] = first[stream, shard]
+    finish(copies)
+    out_ref[stream, shard] = plain_sum(second, sizes["seq"])
+    finish(
+        exchange(
+            "seq",
+            sizes["seq"],
+            lambda p: out_ref.at[stream, shard],
+            lambda m: out_ref.at[stream, m],
+            sem[4],
+            sem[5],
+        )
+    )
+    finish(
+        exchange(
+            "dp",
+            sizes["dp"],
+            lambda p: out_ref.at[stream],
+            lambda m: out_ref.at[m],
+            sem[6],
+            sem[7],
+        )
+    )
+
+
+def wide_reduce(rows, ident):
+    sizes = {axis: lax.axis_size(axis) for axis in AXES}
+    shares = sizes["dp"] * sizes["seq"]
+    flat = rows.reshape(-1, LANES)
+    unit = -(-flat.shape[0] // (shares * 8)) * 8
+    padded = jnp.pad(flat, ((0, shares * unit - flat.shape[0]), (0, 0)))
+    blocks = padded.reshape(sizes["dp"], sizes["seq"], unit, LANES)
+    out = pl.pallas_call(
+        functools.partial(wide_kernel, sizes),
+        out_shape=jax.ShapeDtypeStruct(blocks.shape, jnp.float32),
+        in_specs=[pl.BlockSpec(memory_space=pltpu.VMEM)],
+        out_specs=pl.BlockSpec(memory_space=pltpu.VMEM),
+        scratch_shapes=[
+            pltpu.VMEM(blocks.shape, jnp.float32),
+            pltpu.VMEM(blocks.shape[1:], jnp.float32),
+            *sems(sizes, "dp"),
+            *sems(sizes, "seq"),
+            *sems(sizes, "seq"),
+            *sems(sizes, "dp"),
+        ],
+        compiler_params=pltpu.CompilerParams(collective_id=ident, has_side_effects=True),
+    )(blocks)
+    return out.reshape(-1, LANES)[: flat.shape[0]].reshape(rows.shape)
 
 
 def on_device(
@@ -43,10 +236,19 @@
     conv_out = jnp.zeros((frames, masked.shape[1]), jnp.float32)
     for tap in range(KERNEL):
         conv_out = conv_out + kernel[tap] * padded[tap : tap + frames]
-    total = lax.psum(jnp.sum(jnp.where(valid, conv_out, 0.0), axis=0), ("dp", "seq"))
+    shards = lax.axis_size("seq")
+    held = jnp.clip(lengths[:, None] - frames * jnp.arange(shards)[None], 0, frames)
+    held = held.astype(jnp.float32)
+    own = held[stream, shard]
+    dp_frames = jnp.broadcast_to(held[:, shard][:, None, None], (held.shape[0], 1, LANES))
+    seq_frames = jnp.broadcast_to(jnp.sum(held, axis=0)[:, None, None], (shards, 1, LANES))
+    own_sum = jnp.sum(jnp.where(valid, conv_out, 0.0), axis=0)
+    own_off = jnp.where(valid, conv_out - own_sum / jnp.maximum(own, 1.0), 0.0)
+    own_spread = jnp.sum(own_off * own_off, axis=0)
+    total, spread = small_reduce(
+        jnp.stack([own_sum, own_spread]), 0, (dp_frames, seq_frames)
+    )
     channel_mean = total / count
-    deviation = jnp.where(valid, conv_out - channel_mean, 0.0)
-    spread = lax.psum(jnp.sum(deviation * deviation, axis=0), ("dp", "seq"))
     channel_var = spread / count
     inv_std = lax.rsqrt(channel_var + norm_eps)
     standard = (conv_out - channel_mean) * inv_std
@@ -68,8 +270,8 @@
     )
     module_out = jnp.where(valid, product, 0.0).astype(jnp.bfloat16)
     scaled_grad = hidden_grad * logistic * (1.0 + scaled * (1.0 - logistic))
-    gain_grad, bias_grad = lax.psum(
-        (jnp.sum(scaled_grad * standard, axis=0), jnp.sum(scaled_grad, axis=0)), ("dp", "seq")
+    gain_grad, bias_grad = small_reduce(
+        jnp.stack([jnp.sum(scaled_grad * standard, axis=0), jnp.sum(scaled_grad, axis=0)]), 1
     )
     conv_grad = jnp.where(
         valid,
@@ -85,16 +287,16 @@
     tap_rows = []
     for tap in range(KERNEL):
         tap_rows.append(jnp.sum(conv_grad * padded[tap : tap + frames], axis=0))
-    kernel_grad = lax.psum(jnp.stack(tap_rows), ("dp", "seq"))
+    kernel_grad = wide_reduce(jnp.stack(tap_rows), 2)
     columns = hidden
     weight_grad = lax.psum_scatter(
         lax.dot_general(
             columns, grad_out, (((0,), (0,)), ((), ())), preferred_element_type=jnp.float32
-        ),
+        ).astype(jnp.bfloat16),
         ("dp", "seq"),
         scatter_dimension=0,
         tiled=True,
-    )
+    ).astype(jnp.float32)
     new_one = beta_one * moment_one + (1.0 - beta_one) * weight_grad
     new_two = beta_two * moment_two + (1.0 - beta_two) * weight_grad * weight_grad
     new_master = master - adam_rate * (new_one / first_fix) / (

time: 390 us -> 288 us (0.74)
  blocking collectives: 121 us -> 0 us
  Pallas kernels: 0 us -> 40.8 us
  waiting for transfers between devices: 200 us -> 172 us
    psum x1 -> x0, waiting for transfers between devices: 129 us -> none  [on_device(): kernel_grad = lax.psum(jnp.stack(tap_rows), ('dp', 'seq'))]
    psum x3 -> x0, blocking collectives: 121 us -> none  [the longest x1 41 us: on_device(): lax.psum(jnp.sum(jnp.where(valid, conv_out, 0.0), axis=0), ('dp', 'seq'))]
    all_gather x1, waiting for transfers between devices: 0.02 us -> 64.6 us  [on_device(): lax.all_gather(weight, ('dp', 'seq'), axis=0, tiled=True)]
    pallas_call x0 -> x3, Pallas kernels: none -> 40.8 us  [the longest x2 20.6 us: small_reduce(): pl.pallas_call(functools.partial(small_kernel, sizes, frames is not None)...]
    reduce_scatter x1, waiting for transfers between devices: 69.7 us -> 107 us  [on_device(): lax.psum_scatter(lax.dot_general(columns, grad_out, (((0,), (0,)), ((), (...]
  transfers between devices with their start and end apart: 7 -> 6, of which waited for: 3 -> 2; matrix products, arithmetic and copies ran while one was open for 10% -> 5% of each run, Pallas kernels for 0% -> 7%
where the time goes in v1:
time: 288 us; the launch traced here: 284 us
  waiting for transfers between devices  172 us (60%)
  Pallas kernels  40.8 us (14%)
  other arithmetic  20.8 us (7%)
  between operations  16.1 us (6%)
  starting transfers between devices  13.3 us (5%)
  local copies, waits for them, and re-layouts  11.6 us (4%)
  matrix products  9.48 us (3%)
    reduce_scatter x1, waiting for transfers between devices, on_device(): lax.psum_scatter(lax.dot_general(columns, grad_out, (((0,), (0,)), ((), (...  107 us
    all_gather x1, waiting for transfers between devices, on_device(): lax.all_gather(weight, ('dp', 'seq'), axis=0, tiled=True)  64.6 us
    pallas_call x2, Pallas kernels, small_reduce(): pl.pallas_call(functools.partial(small_kernel, sizes, frames is not None)...  20.6 us
    pallas_call x1, Pallas kernels, wide_reduce(): pl.pallas_call(functools.partial(wide_kernel, sizes), out_shape=jax.Shape...  20.2 us
    ppermute x2, starting transfers between devices, with_halo(): lax.ppermute(lax.slice_in_dim(block, 0, width, axis=dim), axis, backward)  7.57 us
  transfers between devices with their start and end apart: 6, of which 2 were waited for; matrix products, arithmetic and copies ran while one was open for 5% of the time, Pallas kernels for 7%

profile of v1, /device:TPU:10, one launch (start us, length us, event | category | flops | bytes accessed | tf_op | source)
XLA Modules:
  0.0 284.3 jit_solution(14775256214019670956)
XLA Ops:
  7.2 0.0 reduce-scatter.2.cloned.1.call-start
  7.2 1.2 dynamic_slice.9
  8.5 0.7 add_compare_fusion
  9.1 1.1 bitcast_select_fusion.1
  10.2 3.4 %collective-permute-start = (bf16[15,1536]{1,0:T(8,128)(2,1)S(1)}, bf16[15,1536]{1,0:T(8,128)(2,1)S(1)}, u32[]{:S(2)}, u32[]{:S(2)}) collective-permute-start(bf16[15,1536]{1,0:T(8,128)(2,1)S(1)} %get-tuple-element.82), channel_id=1, source_target_pairs={{0,1},{1,2},{2,3},{3,4},{4,5},{5,6},{6,7},{8,9},{9,10},{10,11},{11... | collective-permute-start | bytes 138248 | tf_op jit(solution)/shard_map/ppermute | solution.py:28
  13.7 3.3 %collective-permute-start.1 = (bf16[15,1536]{1,0:T(8,128)(2,1)S(1)}, bf16[15,1536]{1,0:T(8,128)(2,1)S(1)}, u32[]{:S(2)}, u32[]{:S(2)}) collective-permute-start(bf16[15,1536]{1,0:T(8,128)(2,1)S(1)} %get-tuple-element.83), channel_id=1, source_target_pairs={{1,0},{2,1},{3,2},{4,3},{5,4},{6,5},{7,6},{9,8},{10,9},{11,10},{12... | collective-permute-start | bytes 138248 | tf_op jit(solution)/shard_map/ppermute | solution.py:31
  17.0 0.8 fusion.97
  17.9 0.7 clamp_convert_fusion
  18.6 1.5 slice_reduce_fusion.29
  20.2 1.9 slice_reduce_fusion.30
  22.1 1.3 reduce_sum.336
  23.4 0.6 dynamic_slice.10
  25.3 0.1 maximum_convert_fusion
  25.4 0.0 copy-start.14
  25.5 0.0 copy-start.23
  25.5 0.0 copy-start.24
  25.5 3.2 %select_reduce_fusion = (f32[1536]{0:T(1024)S(1)}, f32[128,1536]{1,0:T(8,128)S(1)}) fusion(pred[128]{0:T(512)(128)(4,1)S(1)} %add_compare_fusion, f32[158,1536]{1,0:T(8,128)S(1)} %maximum_convert_fusion, f32[1536]{0:T(1024)S(1)} %get-tuple-element.70, f32[1536]{0:T(1024)S(1)} %get-tuple-element.71, f32[1536]{0:T(1024)S(1)} %get-tuple-element.42, ...), kind=kLoop, calls=%fused_computation.191 | loop fusion | flops 12384768 | bytes 25362560 | tf_op jit(solution)/shard_map/reduce_sum | solution.py:245
  28.7 0.2 multiply_reduce_fusion.32
  28.9 0.6 reshape.89.x_ref
  29.6 0.6 broadcast_in_dim.77.rest_0_
  30.2 0.7 broadcast_in_dim.78.rest_1_
  30.9 10.8 %shard_map.161 = f32[24,128]{1,0:T(8,128)} custom-call(f32[24,128]{1,0:T(8,128)} %reshape.89.x_ref, f32[4,1,128]{2,1,0:T(1,128)} %broadcast_in_dim.77.rest_0_, f32[8,1,128]{2,1,0:T(1,128)} %broadcast_in_dim.78.rest_1_), custom_call_target="tpu_custom_call" | custom-call | tf_op jit(solution)/shard_map/pallas_call | solution.py:142
  41.7 0.8 divide_bitcast_fusion
  42.5 3.6 %convolution_convert_fusion = bf16[1536,1536]{1,0:T(8,128)(2,1)} fusion(bf16[1,128,1536]{2,1,0:T(8,128)(2,1)S(1)} %copy-done.23, pred[128]{0:T(512)(128)(4,1)S(1)} %add_compare_fusion, f32[128,1536]{1,0:T(8,128)S(1)} %get-tuple-element.79, f32[1536]{0:T(1024)S(1)} %copy-done.24, f32[1536]{0:T(1024)S(1)} %get-tuple-element.85, f32[1536]{0:T(1024)S(1)} %get-tuple-element.84, ...), kind=kOutput, calls=%fused_computation | convolution fusion | flops 608305152 | bytes 5922944 | tf_op jit(solution)/shard_map/dot_general | solution.py:293
  46.1 0.0 reduce-scatter.2.cloned.1.call-update
  46.2 0.0 all-gather.2.cloned.1.call-start
  46.2 0.7 all-gather.2.cloned.1.call-update
  46.9 106.9 %reduce-scatter.2.cloned.1.call-done = bf16[48,1536]{1,0:T(8,128)(2,1)} async-done(((bf16[1536,1536]{1,0:T(8,128)(2,1)}), bf16[48,1536]{1,0:T(8,128)(2,1)}) %reduce-scatter.2.cloned.1.call-update) | async-done | bytes 147472 | tf_op jit(solution)/shard_map/reduce_scatter | solution.py:292
  153.8 1.9 divide_subtract_fusion
  155.7 64.6 %all-gather.2.cloned.1.call-done = bf16[1536,1536]{1,0:T(8,128)(2,1)} async-done(((bf16[48,1536]{1,0:T(8,128)(2,1)}), bf16[1536,1536]{1,0:T(8,128)(2,1)}) %all-gather.2.cloned.1.call-update) | async-done | bytes 4718608 | tf_op jit(solution)/shard_map/all_gather | solution.py:262
  220.3 4.2 %multiply_reduce_fusion.31 = (f32[1536]{0:T(1024)S(1)}, f32[1536]{0:T(1024)S(1)}, f32[128,1536]{1,0:T(8,128)S(1)}) fusion(f32[128,1536]{1,0:T(8,128)S(1)} %get-tuple-element.79, f32[1536]{0:T(1024)S(1)} %get-tuple-element.85, f32[1536]{0:T(1024)S(1)} %get-tuple-element.84, f32[1536]{0:T(1024)S(1)} %copy-done.24, f32[1536]{0:T(1024)S(1)} %copy-done.14, ...), kind=kOutput, calls=%fused_computation.186 | convolution fusion | flops 607122432 | bytes 6721664 | tf_op jit(solution)/shard_map/dot_general | solution.py:265
  224.6 0.6 reshape.90.x_ref
  225.2 9.8 %shard_map.162 = f32[24,128]{1,0:T(8,128)} custom-call(f32[24,128]{1,0:T(8,128)} %reshape.90.x_ref), custom_call_target="tpu_custom_call" | custom-call | tf_op jit(solution)/shard_map/pallas_call | solution.py:142
  235.0 0.7 slice_bitcast_fusion
  235.7 1.3 multiply_divide_fusion
  237.0 3.1 %multiply_reduce_fusion = (f32[1536]{0:T(1024)S(1)}, f32[1536]{0:T(1024)S(1)}, f32[1536]{0:T(1024)S(1)}, f32[1536]{0:T(1024)S(1)}, f32[1536]{0:T(1024)S(1)}, /*i...) fusion(f32[158,1536]{1,0:T(8,128)S(1)} %maximum_convert_fusion,, ...), kind=kLoop, calls=%fused_computation.154 | loop fusion | flops 9016320 | bytes 16656516 | tf_op jit(solution)/shard_map/reduce_sum | solution.py:289
  240.1 0.0 copy-start.15
  240.2 0.0 copy-start.25
  240.2 1.2 multiply_reduce_fusion.1
  241.4 4.3 %collective-permute-start.2 = (f32[15,1536]{1,0:T(8,128)S(1)}, f32[15,1536]{1,0:T(8,128)S(1)}, u32[]{:S(2)}, u32[]{:S(2)}) collective-permute-start(f32[15,1536]{1,0:T(8,128)S(1)} %get-tuple-element.80), channel_id=1, source_target_pairs={{1,0},{2,1},{3,2},{4,3},{5,4},{6,5},{7,6},{9,8},{10,9},{11,10},{12... | collective-permute-start | bytes 276488 | tf_op jit(solution)/shard_map/ppermute | solution.py:31
  245.7 2.2 collective-permute-start.3
  248.0 1.6 fusion.2
  250.1 0.3 stack.151
  250.4 0.7 pad.4
  251.1 20.2 %shard_map.163 = f32[4,8,16,128]{3,2,1,0:T(8,128)} custom-call(f32[4,8,16,128]{3,2,1,0:T(8,128)} %bitcast.29), custom_call_target="tpu_custom_call" | custom-call | tf_op jit(solution)/shard_map/pallas_call | solution.py:207
  271.4 0.9 slice.575
  272.3 0.7 reshape.94
  273.1 4.4 %fusion.94 = bf16[1,128,1536]{2,1,0:T(8,128)(2,1)} fusion(f32[128,1536]{1,0:T(8,128)S(1)} %get-tuple-element.75, f32[15,1536]{1,0:T(8,128)S(1)} %collective-permute-done.3, f32[1536]{0:T(1024)S(1)} %copy-done.10, f32[1536]{0:T(1024)S(1)} %copy-done.12, f32[1536]{0:T(1024)S(1)} %get-tuple-element.42, f32[1536]{0:T(1024)S(1)} %get-tuple-element.43, ...), kind=kLoop, calls=%fused_computation.198 | loop fusion | flops 18284544 | bytes 1554560 | tf_op jit(solution)/shard_map/broadcast_in_dim | solution.py:307
  (94 shorter events, 0.4 us)
Async XLA Ops:
  7.2 146.6 %reduce-scatter.2.cloned.1.call-start = ((), (), s32[]{:S(2)}) async-start(), calls=%async_computation.2 | async-start | bytes 4866048 | tf_op jit(solution)/shard_map/reduce_scatter | solution.py:292
  9.1 211.2 %copy-start.20 = (pred[128]{0:T(512)(128)(4,1)}, pred[128]{0:T(512)(128)(4,1)S(1)}, u32[]{:S(2)}) copy-start(pred[128]{0:T(512)(128)(4,1)S(1)} %add_compare_fusion) | copy-start | bytes 388
  10.2 15.0 %collective-permute-start = (bf16[15,1536]{1,0:T(8,128)(2,1)S(1)}, bf16[15,1536]{1,0:T(8,128)(2,1)S(1)}, u32[]{:S(2)}, u32[]{:S(2)}) collective-permute-start(bf16[15,1536]{1,0:T(8,128)(2,1)S(1)} %get-tuple-element.82), channel_id=1, source_target_pairs={{0,1},{1,2},{2,3},{3,4},{4,5},{5,6},{6,7},{8,9},{9,10},{10,11},{11... | collective-permute-start | bytes 138248 | tf_op jit(solution)/shard_map/ppermute | solution.py:28
  13.7 11.6 %collective-permute-start.1 = (bf16[15,1536]{1,0:T(8,128)(2,1)S(1)}, bf16[15,1536]{1,0:T(8,128)(2,1)S(1)}, u32[]{:S(2)}, u32[]{:S(2)}) collective-permute-start(bf16[15,1536]{1,0:T(8,128)(2,1)S(1)} %get-tuple-element.83), channel_id=1, source_target_pairs={{1,0},{2,1},{3,2},{4,3},{5,4},{6,5},{7,6},{9,8},{10,9},{11,10},{12... | collective-permute-start | bytes 138248 | tf_op jit(solution)/shard_map/ppermute | solution.py:31
  20.1 8.5 %copy-start.3 = (f32[1536]{0:T(1024)}, f32[1536]{0:T(1024)S(1)}, u32[]{:S(2)}) copy-start(f32[1536]{0:T(1024)S(1)} %get-tuple-element.67) | copy-start | bytes 18436
  20.1 8.5 %copy-start.5 = (f32[1536]{0:T(1024)}, f32[1536]{0:T(1024)S(1)}, u32[]{:S(2)}) copy-start(f32[1536]{0:T(1024)S(1)} %get-tuple-element.68) | copy-start | bytes 18436
  20.1 8.5 %copy-start.7 = (f32[1536]{0:T(1024)}, f32[1536]{0:T(1024)S(1)}, u32[]{:S(2)}) copy-start(f32[1536]{0:T(1024)S(1)} %get-tuple-element.69) | copy-start | bytes 18436
  20.1 8.5 %copy-start.9 = (f32[1536]{0:T(1024)}, f32[1536]{0:T(1024)S(1)}, u32[]{:S(2)}) copy-start(f32[1536]{0:T(1024)S(1)} %get-tuple-element.70) | copy-start | bytes 18436
  20.2 8.5 %copy-start.11 = (f32[1536]{0:T(1024)}, f32[1536]{0:T(1024)S(1)}, u32[]{:S(2)}) copy-start(f32[1536]{0:T(1024)S(1)} %get-tuple-element.71) | copy-start | bytes 18436
  25.4 17.0 %copy-start.14 = (f32[1536]{0:T(1024)S(1)}, f32[1536]{0:T(1024)}, u32[]{:S(2)}) copy-start(f32[1536]{0:T(1024)} %param.13) | copy-start | bytes 18436
  25.5 17.0 %copy-start.23 = (bf16[1,128,1536]{2,1,0:T(8,128)(2,1)S(1)}, bf16[1,128,1536]{2,1,0:T(8,128)(2,1)}, u32[]{:S(2)}) copy-start(bf16[1,128,1536]{2,1,0:T(8,128)(2,1)} %param.19) | copy-start | bytes 1179652
  25.5 17.0 %copy-start.24 = (f32[1536]{0:T(1024)S(1)}, f32[1536]{0:T(1024)}, u32[]{:S(2)}) copy-start(f32[1536]{0:T(1024)} %param.14) | copy-start | bytes 18436
  42.5 177.9 %copy-start.16 = (f32[1536]{0:T(1024)}, f32[1536]{0:T(1024)S(1)}, u32[]{:S(2)}) copy-start(f32[1536]{0:T(1024)S(1)} %get-tuple-element.84) | copy-start | bytes 18436
  42.5 177.9 %copy-start.18 = (f32[1536]{0:T(1024)}, f32[1536]{0:T(1024)S(1)}, u32[]{:S(2)}) copy-start(f32[1536]{0:T(1024)S(1)} %get-tuple-element.85) | copy-start | bytes 18436
  46.1 107.6 %copy-start = (f32[48,1536]{1,0:T(8,128)S(1)}, f32[48,1536]{1,0:T(8,128)}, u32[]{:S(2)}) copy-start(f32[48,1536]{1,0:T(8,128)} %param.16) | copy-start | bytes 884740
  46.1 107.6 %copy-start.1 = (f32[48,1536]{1,0:T(8,128)S(1)}, f32[48,1536]{1,0:T(8,128)}, u32[]{:S(2)}) copy-start(f32[48,1536]{1,0:T(8,128)} %param.17) | copy-start | bytes 884740
  46.1 107.6 %copy-start.2 = (f32[48,1536]{1,0:T(8,128)S(1)}, f32[48,1536]{1,0:T(8,128)}, u32[]{:S(2)}) copy-start(f32[48,1536]{1,0:T(8,128)} %param.18) | copy-start | bytes 884740
  46.2 174.1 %all-gather.2.cloned.1.call-start = ((), (), s32[]{:S(2)}) async-start(), calls=%async_computation.1 | async-start | bytes 4866048 | tf_op jit(solution)/shard_map/all_gather | solution.py:262
  235.7 4.4 %copy-start.13 = (f32[1536]{0:T(1024)}, f32[1536]{0:T(1024)S(1)}, u32[]{:S(2)}) copy-start(f32[1536]{0:T(1024)S(1)} %slice_bitcast_fusion) | copy-start | bytes 18436
  240.1 7.8 %copy-start.15 = (f32[1536]{0:T(1024)S(1)}, f32[1536]{0:T(1024)}, u32[]{:S(2)}) copy-start(f32[1536]{0:T(1024)} %param.13) | copy-start | bytes 18436
  240.1 7.8 %copy-start.17 = (f32[1536]{0:T(1024)S(1)}, f32[1536]{0:T(1024)}, u32[]{:S(2)}) copy-start(f32[1536]{0:T(1024)} %copy-done.16) | copy-start | bytes 18436
  240.1 7.8 %copy-start.19 = (f32[1536]{0:T(1024)S(1)}, f32[1536]{0:T(1024)}, u32[]{:S(2)}) copy-start(f32[1536]{0:T(1024)} %copy-done.18) | copy-start | bytes 18436
  240.1 7.8 %copy-start.21 = (pred[128]{0:T(512)(128)(4,1)S(1)}, pred[128]{0:T(512)(128)(4,1)}, u32[]{:S(2)}) copy-start(pred[128]{0:T(512)(128)(4,1)} %copy-done.20) | copy-start | bytes 388
  240.1 7.8 %copy-start.22 = (bf16[1536,1536]{1,0:T(8,128)(2,1)S(1)}, bf16[1536,1536]{1,0:T(8,128)(2,1)}, u32[]{:S(2)}) copy-start(bf16[1536,1536]{1,0:T(8,128)(2,1)} %all-gather.2.cloned.1.call-done) | copy-start | bytes 14155780
  240.2 7.8 %copy-start.25 = (f32[1536]{0:T(1024)S(1)}, f32[1536]{0:T(1024)}, u32[]{:S(2)}) copy-start(f32[1536]{0:T(1024)} %param.14) | copy-start | bytes 18436
  241.4 31.6 %collective-permute-start.2 = (f32[15,1536]{1,0:T(8,128)S(1)}, f32[15,1536]{1,0:T(8,128)S(1)}, u32[]{:S(2)}, u32[]{:S(2)}) collective-permute-start(f32[15,1536]{1,0:T(8,128)S(1)} %get-tuple-element.80), channel_id=1, source_target_pairs={{1,0},{2,1},{3,2},{4,3},{5,4},{6,5},{7,6},{9,8},{10,9},{11,10},{12... | collective-permute-start | bytes 276488 | tf_op jit(solution)/shard_map/ppermute | solution.py:31
  245.7 27.4 %copy-start.4 = (f32[1536]{0:T(1024)S(1)}, f32[1536]{0:T(1024)}, u32[]{:S(2)}) copy-start(f32[1536]{0:T(1024)} %copy-done.3) | copy-start | bytes 18436
  245.7 27.4 %copy-start.6 = (f32[1536]{0:T(1024)S(1)}, f32[1536]{0:T(1024)}, u32[]{:S(2)}) copy-start(f32[1536]{0:T(1024)} %copy-done.5) | copy-start | bytes 18436
  245.7 27.4 %copy-start.8 = (f32[1536]{0:T(1024)S(1)}, f32[1536]{0:T(1024)}, u32[]{:S(2)}) copy-start(f32[1536]{0:T(1024)} %copy-done.7) | copy-start | bytes 18436
  245.7 27.4 %copy-start.10 = (f32[1536]{0:T(1024)S(1)}, f32[1536]{0:T(1024)}, u32[]{:S(2)}) copy-start(f32[1536]{0:T(1024)} %copy-done.9) | copy-start | bytes 18436
  245.7 27.4 %copy-start.12 = (f32[1536]{0:T(1024)S(1)}, f32[1536]{0:T(1024)}, u32[]{:S(2)}) copy-start(f32[1536]{0:T(1024)} %copy-done.11) | copy-start | bytes 18436
  245.7 27.3 %collective-permute-start.3 = (f32[15,1536]{1,0:T(8,128)S(1)}, f32[15,1536]{1,0:T(8,128)S(1)}, u32[]{:S(2)}, u32[]{:S(2)}) collective-permute-start(f32[15,1536]{1,0:T(8,128)S(1)} %get-tuple-element.81), channel_id=1, source_target_pairs={{0,1},{1,2},{2,3},{3,4},{4,5},{5,6},{6,7},{8,9},{9,10},{10,11},{11... | collective-permute-start | bytes 276488 | tf_op jit(solution)/shard_map/ppermute | solution.py:28
Sparse Core Ops, SparseCore 0:
  46.3 107.4 reduce-scatter.1
  157.1 63.1 all-gather.1
